TPU v7x, 512 devices: a whole 4x8x8 slice. The times are simulated.
512 devices in a mesh: grp: 2 (over core), seq: 128 (over z_hi, x, y), dp: 2 (over z_lo).
Axes of the slice: x: 4, y: 8, z: 8 (z_hi: 4, z_lo: 2; z = z_hi * 2 + z_lo), core: 2. Of those that a mesh axis runs over, the one named last changes fastest.
Arguments:
- qkv: bfloat16 [2, 3, 2, 22528, 1536], P('grp', None, 'dp', 'seq'), may hold values from -4.5 to 4.5
- cotangent: bfloat16 [2, 2, 22528, 1536], P('grp', 'dp', 'seq'), may hold values from -4 to 4
- gate: float32 [1536], replicated, may hold values from 0.5 to 2
- tile_map: int32 [2, 32, 704], P('dp'), may hold values from 0 to 703, as said below
- text_count: int32 [2, 32], P('dp'), may hold values from 1 to 128
Outputs:
- blended: bfloat16 [2, 2, 22528, 1536], P('grp', 'dp', 'seq')
- input_grads: bfloat16 [2, 3, 2, 22528, 1536], P('grp', None, 'dp', 'seq')
- gate_grad: float32 [1536], replicated
Inputs may be any that keep to these rules, and one draw needn't show every extreme that they name: `tile_map`: each row keeps positions below 128 in place and lists the image tokens tile by tile, 4 x 4 tokens a tile, of an image 24 tokens a side; every row is a permutation.
All inputs are finite; a program needn't handle non-finite values.
Results may differ from a plain program's by a relative error of at most 0.0062.
Values may be sent and summed in bfloat16 or wider, within the bound.
A program may use at most 64 MiB of HBM per device.

v0:
```python
import math

import jax
import jax.numpy as jnp
from jax import lax
from jax.sharding import PartitionSpec as P

HEADS = 12
HD = 128
GROUP = 4
TXT = 128


def swapped(value, axis, distance):
    mask = 2**distance
    pairs = [(source, source ^ mask) for source in range(lax.axis_size(axis))]
    return lax.ppermute(value, axis, pairs)


def exchange_cube(blocks, member, sender):
    ordering = jnp.bitwise_xor(member, jnp.arange(GROUP, dtype=jnp.int32))
    held = jnp.take(blocks, ordering, axis=0)
    for bit_level in range(GROUP.bit_length() - 1):
        stride = 1 << bit_level
        shaped = held.reshape((GROUP // (2 * stride), 2, stride) + held.shape[1:])
        arrived = sender(shaped[:, 1], bit_level)
        held = jnp.stack([shaped[:, 0], arrived], axis=1).reshape(held.shape)
    return jnp.take(held, ordering, axis=0)


def to_heads(tensors, member):
    number, row_count, channels = tensors.shape
    head_share = HEADS // GROUP
    blocks = tensors.reshape(number, row_count, GROUP, head_share, HD).transpose(2, 0, 3, 1, 4)
    arrived = exchange_cube(
        blocks, member, lambda portion, bit_level: swapped(portion, "seq", bit_level)
    )
    return arrived.transpose(1, 2, 0, 3, 4).reshape(number, head_share, GROUP * row_count, HD)


def to_tokens(tensors, member):
    number, head_share, length, head_dim = tensors.shape
    row_count = length // GROUP
    blocks = tensors.reshape(number, head_share, GROUP, row_count, head_dim).transpose(
        2, 0, 1, 3, 4
    )
    arrived = exchange_cube(
        blocks, member, lambda portion, bit_level: swapped(portion, "seq", bit_level)
    )
    return arrived.transpose(1, 3, 0, 2, 4).reshape(
        number, row_count, GROUP * head_share * head_dim
    )


def gather_rows(rows_in, member):
    gathered = rows_in
    for bit_level in range(GROUP.bit_length() - 1):
        partner = swapped(gathered, "seq", bit_level)
        upper = member >> bit_level & 1
        gathered = jnp.where(
            upper == 1,
            jnp.concatenate([partner, gathered], axis=0),
            jnp.concatenate([gathered, partner], axis=0),
        )
    return gathered


def pass_rows(tensor):
    return swapped(tensor, "grp", 0)


def attend_heads(queries, keys_in, values, out_grad, usable):
    head_share, length, head_dim = queries.shape
    half_rows = length // 2
    score_scale = 1.0 / math.sqrt(head_dim)

    def split_rows(tensor):
        return tensor.reshape(head_share, 2, half_rows, head_dim).transpose(1, 0, 2, 3)

    def join_rows(tensor):
        return tensor.transpose(1, 0, 2, 3).reshape(head_share, length, head_dim)

    def advance(running, portion):
        query_part, grad_part = portion
        scores = (
            jnp.einsum("hqd,hkd->hqk", query_part, keys_in, preferred_element_type=jnp.float32)
            * score_scale
        )
        scores = jnp.where(usable[None, None, :], scores, -jnp.inf)
        attn_probs = jax.nn.softmax(scores, axis=-1)
        probs_low = attn_probs.astype(jnp.bfloat16)
        output = jnp.einsum("hqk,hkd->hqd", probs_low, values, preferred_element_type=jnp.float32)
        grad_probs = jnp.einsum(
            "hqd,hkd->hqk", grad_part, values, preferred_element_type=jnp.float32
        )
        centre = jnp.sum(attn_probs * grad_probs, axis=-1, keepdims=True)
        shifted = (attn_probs * (grad_probs - centre)).astype(jnp.bfloat16)
        query_grad = (
            jnp.einsum("hqk,hkd->hqd", shifted, keys_in, preferred_element_type=jnp.float32)
            * score_scale
        )
        key_sum = (
            running[0]
            + jnp.einsum("hqk,hqd->hkd", shifted, query_part, preferred_element_type=jnp.float32)
            * score_scale
        )
        value_sum = running[1] + jnp.einsum(
            "hqk,hqd->hkd", probs_low, grad_part, preferred_element_type=jnp.float32
        )
        return ((key_sum, value_sum), (output, query_grad))

    empty_sum = jnp.zeros((head_share, length, head_dim), jnp.float32)
    sums, pieces = lax.scan(
        advance, (empty_sum, empty_sum), (split_rows(queries), split_rows(out_grad))
    )
    return (join_rows(pieces[0]), join_rows(pieces[1]), sums[0], sums[1])


def per_device(qkv, cotangent, gate, tile_map, text_count):
    branch = lax.axis_index("grp")
    position = lax.axis_index("seq")
    member = position % GROUP
    sequence = position // GROUP
    row_count = qkv.shape[3]
    length = row_count * GROUP
    control = branch == 0
    ordering = lax.dynamic_index_in_dim(tile_map[0], sequence, 0, keepdims=False)
    counted = lax.dynamic_index_in_dim(text_count[0], sequence, 0, keepdims=False)
    inverse = jnp.zeros((length,), jnp.int32).at[ordering].set(jnp.arange(length, dtype=jnp.int32))
    places = jnp.arange(length, dtype=jnp.int32)
    usable = (places >= TXT) | (places < counted)
    inputs = qkv[0, :, 0]
    upstream = cotangent[0, 0]
    shared = gather_rows(upstream, member)
    wanted = lax.dynamic_slice_in_dim(ordering, member * row_count, row_count)
    returned = pass_rows(jnp.take(shared, wanted, axis=0)).astype(jnp.float32)
    mixed_grad = (upstream.astype(jnp.float32) + gate[None, :] * returned).astype(jnp.bfloat16)
    out_grad = jnp.where(control, mixed_grad, upstream)
    heads = to_heads(jnp.concatenate([inputs, out_grad[None]], axis=0), member)
    head_grad = heads[3]
    attended, query_grad, key_grad, value_grad = attend_heads(
        heads[0], heads[1], heads[2], head_grad, usable
    )
    attn_out = attended.astype(jnp.bfloat16)
    grads = jnp.stack([query_grad, key_grad, value_grad]).astype(jnp.bfloat16)
    back_tokens = to_tokens(jnp.concatenate([attn_out[None], grads], axis=0), member)
    own_out = back_tokens[0]
    scaled = (gate[None, :] * own_out.astype(jnp.float32)).astype(jnp.bfloat16)
    shared_out = gather_rows(scaled, member)
    wanted_out = lax.dynamic_slice_in_dim(inverse, member * row_count, row_count)
    arriving = pass_rows(jnp.take(shared_out, wanted_out, axis=0))
    blended = jnp.where(
        control,
        own_out,
        (own_out.astype(jnp.float32) + arriving.astype(jnp.float32)).astype(jnp.bfloat16),
    )
    partial_sum = jnp.sum(own_out.astype(jnp.float32) * returned, axis=0)
    partial_sum = jnp.where(control, partial_sum, jnp.zeros_like(partial_sum))
    gate_grad = lax.psum(partial_sum, ("grp", "seq", "dp"))
    grad_tokens = back_tokens[1:]
    return (blended[None, None], grad_tokens[None, :, None], gate_grad)


def solution(mesh):
    placed = (
        P("grp", None, "dp", "seq", None),
        P("grp", "dp", "seq", None),
        P(),
        P("dp", None, None),
        P("dp", None),
    )
    return jax.shard_map(
        per_device,
        mesh=mesh,
        in_specs=placed,
        out_specs=(P("grp", "dp", "seq", None), P("grp", None, "dp", "seq", None), P()),
        check_vma=False,
    )
```

profile of v0, /device:TPU:1, one launch (start us, length us, event | category | flops | bytes accessed | tf_op | source)
XLA Modules:
  0.0 493.6 jit_solution(2973951359810099817)
XLA Ops:
  0.6 4.0 collective-permute-start
  4.7 7.7 %collective-permute-done = bf16[176,1536]{1,0:T(8,128)(2,1)S(1)} collective-permute-done((bf16[176,1536]{1,0:T(8,128)(2,1)}, bf16[176,1536]{1,0:T(8,128)(2,1)S(1)}, u32[]{:S(2)}, u32[]{:S(2)}) %collective-permute-start) | collective-permute-done | bytes 540704 | tf_op jit(solution)/shard_map/ppermute | solution.py:17
  12.4 1.6 maximum_select_fusion.2
  14.0 8.5 %collective-permute-start.1 = (bf16[352,1536]{1,0:T(8,128)(2,1)S(1)}, bf16[352,1536]{1,0:T(8,128)(2,1)}, u32[]{:S(2)}, u32[]{:S(2)}) collective-permute-start(bf16[352,1536]{1,0:T(8,128)(2,1)S(1)} %maximum_select_fusion.2), channel_id=1, source_target_pairs={{0,4},{2,6},{4,0},{6,2},{8,12},{10,14},{12,8},{14,10},{16,20},{18,... | collective-permute-start | bytes 3244040 | tf_op jit(solution)/shard_map/ppermute | solution.py:17
  23.4 45.5 %collective-permute-done.1 = bf16[352,1536]{1,0:T(8,128)(2,1)} collective-permute-done((bf16[352,1536]{1,0:T(8,128)(2,1)S(1)}, bf16[352,1536]{1,0:T(8,128)(2,1)}, u32[]{:S(2)}, u32[]{:S(2)}) %collective-permute-start.1) | collective-permute-done | bytes 1081376 | tf_op jit(solution)/shard_map/ppermute | solution.py:17
  68.9 2.3 maximum_select_fusion
  72.4 3.8 collective-permute-start.2
  76.2 5.7 %concatenate.39 = bf16[3,176,4,3,128]{4,3,2,1,0:T(4,128)(2,1)} reshape(bf16[1,3,1,176,1536]{4,3,2,1,0:T(8,128)(2,1)} %param.11) | data formatting | bytes 3244032 | tf_op jit(solution)/shard_map/concatenate | solution.py:139
  82.8 1.2 concatenate.44
  84.0 3.8 maximum_bitcast_fusion
  87.8 5.2 %gather_fusion.1 = bf16[4,4,3,176,128]{4,2,3,1,0:T(4,128)(2,1)} fusion(bf16[4,4,3,176,128]{4,2,0,3,1:T(4,128)(2,1)S(1)} %maximum_bitcast_fusion, s32[1024]{0:T(1024)S(1)} %pad_clamp_fusion.1), kind=kCustom, calls=%fused_computation.1.clone | custom fusion | bytes 4325392 | tf_op jit(solution)/shard_map/jit(_take)/gather | solution.py:22
  93.0 3.1 broadcast_select_fusion
  96.2 1.1 fusion.59
  97.4 2.4 collective-permute-start.3
  100.0 24.8 %collective-permute-done.3 = bf16[2,1,4,3,176,128]{5,4,3,2,0,1:T(8,128)(2,1)S(1)} collective-permute-done((bf16[2,1,4,3,176,128]{5,4,3,2,0,1:T(8,128)(2,1)S(1)}, bf16[2,1,4,3,176,128]{5,4,3,2,0,1:T(8,128)(2,1)S(1)}, u32[]{:S(2)}, u32[]{:S(2)}) %collective-permute-start.3) | collective-permute-done | bytes 1081376 | tf_op jit(solution)/shard_map/ppermute | solution.py:17
  125.1 4.2 collective-permute-start.4
  130.0 45.9 %collective-permute-done.4 = bf16[1,2,4,3,176,128]{5,4,3,2,1,0:T(8,128)(2,1)S(1)} collective-permute-done((bf16[1,2,4,3,176,128]{5,4,3,2,1,0:T(8,128)(2,1)S(1)}, bf16[1,2,4,3,176,128]{5,4,3,2,1,0:T(8,128)(2,1)S(1)}, u32[]{:S(2)}, u32[]{:S(2)}) %collective-permute-start.4) | collective-permute-done | bytes 1081376 | tf_op jit(solution)/shard_map/ppermute | solution.py:17
  176.9 1.4 pad_maximum_fusion
  178.4 2.2 gather_fusion.2
  180.6 1.9 select_bitcast_fusion.1
  186.0 30.8 %while.17 = (s32[]{:T(128)}, f32[3,704,128]{2,1,0:T(8,128)}, f32[3,704,128]{2,1,0:T(8,128)}, bf16[2,3,352,128]{3,2,0,1:T(8,128)(2,1)}, bf16[2,3,352,128]{3,2,0,1...) while((s32[]{:T(128)}, f32[3,704,128]{2,1,0:T(8,128)}, ...), condition=%wide.region_4.7_spmd.clone, body=%wide.region_0.0_spmd.clone.sunk | while | flops 1154539264 | bytes 93167152 | solution.py:113
  186.6 2.4 fusion.99
  189.1 2.5 multiply_reduce_fusion.2
  191.6 2.5 multiply_convert_fusion.2
  197.5 1.4 convolution_add_fusion.2
  202.0 2.4 fusion.99
  204.5 2.5 multiply_reduce_fusion.2
  207.0 2.5 multiply_convert_fusion.2
  212.9 1.4 convolution_add_fusion.2
  216.8 1.5 convert.14
  218.9 2.2 gather_fusion.3
  221.1 1.9 broadcast_select_fusion.1
  223.2 3.2 collective-permute-start.5
  226.4 22.7 %collective-permute-done.5 = bf16[2,1,4,3,176,128]{5,4,3,2,0,1:T(8,128)(2,1)S(1)} collective-permute-done((bf16[2,1,4,3,176,128]{5,4,3,2,0,1:T(8,128)(2,1)S(1)}, bf16[2,1,4,3,176,128]{5,4,3,2,0,1:T(8,128)(2,1)S(1)}, u32[]{:S(2)}, u32[]{:S(2)}) %collective-permute-start.5) | collective-permute-done | bytes 1081376 | tf_op jit(solution)/shard_map/ppermute | solution.py:17
  249.5 6.1 %collective-permute-start.6 = (bf16[1,2,4,3,176,128]{5,4,3,2,1,0:T(8,128)(2,1)S(1)}, bf16[1,2,4,3,176,128]{5,4,3,2,1,0:T(8,128)(2,1)S(1)}, u32[]{:S(2)}, u32[]{:S(2)}) collective-permute-start(bf16[1,2,4,3,176,128]{5,4,3,2,1,0:T(8,128)(2,1)S(1)} %get-tuple-element.155), channel_id=1, source_target_pairs={{0,4},{2,6},{4,0},{6,2},{8,12},{10,14},{12,8},{14,10},{16,20},{18,... | collective-permute-start | bytes 3244040 | tf_op jit(solution)/shard_map/ppermute | solution.py:17
  255.5 46.6 %collective-permute-done.6 = bf16[1,2,4,3,176,128]{5,4,3,2,1,0:T(8,128)(2,1)S(1)} collective-permute-done((bf16[1,2,4,3,176,128]{5,4,3,2,1,0:T(8,128)(2,1)S(1)}, bf16[1,2,4,3,176,128]{5,4,3,2,1,0:T(8,128)(2,1)S(1)}, u32[]{:S(2)}, u32[]{:S(2)}) %collective-permute-start.6) | collective-permute-done | bytes 1081376 | tf_op jit(solution)/shard_map/ppermute | solution.py:17
  302.3 2.2 gather_fusion.4
  304.5 1.9 select_bitcast_fusion
  306.4 1.4 copy-done.6
  309.1 3.1 collective-permute-start.7
  312.2 11.1 %collective-permute-done.7 = bf16[176,1536]{1,0:T(8,128)(2,1)S(1)} collective-permute-done((bf16[176,1536]{1,0:T(8,128)(2,1)S(1)}, bf16[176,1536]{1,0:T(8,128)(2,1)S(1)}, u32[]{:S(2)}, u32[]{:S(2)}) %collective-permute-start.7) | collective-permute-done | bytes 540704 | tf_op jit(solution)/shard_map/ppermute | solution.py:17
  323.7 6.2 %collective-permute-start.8 = (bf16[352,1536]{1,0:T(8,128)(2,1)S(1)}, bf16[352,1536]{1,0:T(8,128)(2,1)}, u32[]{:S(2)}, u32[]{:S(2)}) collective-permute-start(bf16[352,1536]{1,0:T(8,128)(2,1)S(1)} %maximum_select_fusion.3), channel_id=1, source_target_pairs={{0,4},{2,6},{4,0},{6,2},{8,12},{10,14},{12,8},{14,10},{16,20},{18,... | collective-permute-start | bytes 3244040 | tf_op jit(solution)/shard_map/ppermute | solution.py:17
  330.7 4.1 scatter_custom_fusion
  334.9 41.5 %collective-permute-done.8 = bf16[352,1536]{1,0:T(8,128)(2,1)} collective-permute-done((bf16[352,1536]{1,0:T(8,128)(2,1)S(1)}, bf16[352,1536]{1,0:T(8,128)(2,1)}, u32[]{:S(2)}, u32[]{:S(2)}) %collective-permute-start.8) | collective-permute-done | bytes 1081376 | tf_op jit(solution)/shard_map/ppermute | solution.py:17
  376.4 2.9 maximum_select_fusion.1
  381.3 3.3 collective-permute-start.9
  385.4 2.5 broadcast_in_dim.60
  388.0 104.7 %psum.7 = f32[1536]{0:T(1024)} all-reduce(f32[1536]{0:T(1024)S(1)} %broadcast_select_fusion.4), channel_id=1, replica_groups=mesh['grp'=2,'seq'=128,'dp'=2] {'grp','seq','dp'}, use_global_device_ids=true, to_apply=%region_7.10 | all-reduce | flops 1536 | bytes 12288 | tf_op jit(solution)/shard_map/psum | solution.py:159
  (135 shorter events, 29.0 us)
Async XLA Ops:
  0.6 128.7 %copy-start = (s32[1,32]{1,0:T(1,128)S(1)}, s32[1,32]{1,0:T(1,128)}, u32[]{:S(2)}) copy-start(s32[1,32]{1,0:T(1,128)} %param.15) | copy-start | bytes 388
  0.6 11.8 %collective-permute-start = (bf16[176,1536]{1,0:T(8,128)(2,1)}, bf16[176,1536]{1,0:T(8,128)(2,1)S(1)}, u32[]{:S(2)}, u32[]{:S(2)}) collective-permute-start(bf16[176,1536]{1,0:T(8,128)(2,1)} %bitcast.134), channel_id=1, source_target_pairs={{0,2},{2,0},{4,6},{6,4},{8,10},{10,8},{12,14},{14,12},{16,18},{18,... | collective-permute-start | bytes 1622024 | tf_op jit(solution)/shard_map/ppermute | solution.py:17
  14.0 54.9 %collective-permute-start.1 = (bf16[352,1536]{1,0:T(8,128)(2,1)S(1)}, bf16[352,1536]{1,0:T(8,128)(2,1)}, u32[]{:S(2)}, u32[]{:S(2)}) collective-permute-start(bf16[352,1536]{1,0:T(8,128)(2,1)S(1)} %maximum_select_fusion.2), channel_id=1, source_target_pairs={{0,4},{2,6},{4,0},{6,2},{8,12},{10,14},{12,8},{14,10},{16,20},{18,... | collective-permute-start | bytes 3244040 | tf_op jit(solution)/shard_map/ppermute | solution.py:17
  72.3 9.6 %copy-start.11 = (bf16[1,1,176,1536]{3,2,1,0:T(8,128)(2,1)S(1)}, bf16[1,1,176,1536]{3,2,1,0:T(8,128)(2,1)}, u32[]{:S(2)}) copy-start(bf16[1,1,176,1536]{3,2,1,0:T(8,128)(2,1)} %param.12) | copy-start | bytes 1622020
  72.4 9.6 %copy-start.25 = (f32[1536]{0:T(1024)S(1)}, f32[1536]{0:T(1024)}, u32[]{:S(2)}) copy-start(f32[1536]{0:T(1024)} %param.13) | copy-start | bytes 18436
  72.4 9.5 %collective-permute-start.2 = (bf16[176,1536]{1,0:T(8,128)(2,1)S(1)}, bf16[176,1536]{1,0:T(8,128)(2,1)S(1)}, u32[]{:S(2)}, u32[]{:S(2)}) collective-permute-start(bf16[176,1536]{1,0:T(8,128)(2,1)S(1)} %broadcast_select_fusion.3), channel_id=1, source_target_pairs={{0,256},{256,0},{1,257},{257,1},{2,258},{258,2},{3,259},{259,3},{4... | collective-permute-start | bytes 1622024 | tf_op jit(solution)/shard_map/ppermute | solution.py:17
  81.9 0.8 copy-start.9
  97.4 27.4 %collective-permute-start.3 = (bf16[2,1,4,3,176,128]{5,4,3,2,0,1:T(8,128)(2,1)S(1)}, bf16[2,1,4,3,176,128]{5,4,3,2,0,1:T(8,128)(2,1)S(1)}, u32[]{:S(2)}, u32[]{:S(2)}) collective-permute-start(bf16[2,1,4,3,176,128]{5,4,3,2,0,1:T(8,128)(2,1)S(1)} %bitcast.137), channel_id=1, source_target_pairs={{0,2},{2,0},{4,6},{6,4},{8,10},{10,8},{12,14},{14,12},{16,18},{18,... | collective-permute-start | bytes 3244040 | tf_op jit(solution)/shard_map/ppermute | solution.py:17
  125.1 50.8 %collective-permute-start.4 = (bf16[1,2,4,3,176,128]{5,4,3,2,1,0:T(8,128)(2,1)S(1)}, bf16[1,2,4,3,176,128]{5,4,3,2,1,0:T(8,128)(2,1)S(1)}, u32[]{:S(2)}, u32[]{:S(2)}) collective-permute-start(bf16[1,2,4,3,176,128]{5,4,3,2,1,0:T(8,128)(2,1)S(1)} %get-tuple-element.163), channel_id=1, source_target_pairs={{0,4},{2,6},{4,0},{6,2},{8,12},{10,14},{12,8},{14,10},{16,20},{18,... | collective-permute-start | bytes 3244040 | tf_op jit(solution)/shard_map/ppermute | solution.py:17
  175.9 1.0 copy-start.15
  189.0 2.5 copy-start.2
  191.5 2.6 copy-start.4
  191.6 2.6 copy-start.7
  194.1 1.1 copy-start.19
  194.1 1.2 copy-start.22
  194.1 2.7 copy-start.3
  195.2 3.7 copy-start.5
  195.2 2.1 copy-start.12
  195.2 2.3 copy-start.23
  197.5 2.4 copy-start.16
  197.5 2.4 copy-start.24
  198.9 1.0 copy-start.13
  204.5 2.5 copy-start.2
  206.9 2.6 copy-start.4
  207.0 2.6 copy-start.7
  209.5 1.1 copy-start.19
  209.5 1.2 copy-start.22
  209.6 2.7 copy-start.3
  210.6 3.6 copy-start.5
  210.6 2.1 copy-start.12
  210.6 2.3 copy-start.23
  211.4 0.8 copy-start.20
  212.9 2.4 copy-start.16
  212.9 2.4 copy-start.24
  214.3 1.0 copy-start.13
  216.8 1.6 copy-start.14
  216.8 1.7 copy-start.18
  216.8 1.9 copy-start.21
  223.2 25.9 %collective-permute-start.5 = (bf16[2,1,4,3,176,128]{5,4,3,2,0,1:T(8,128)(2,1)S(1)}, bf16[2,1,4,3,176,128]{5,4,3,2,0,1:T(8,128)(2,1)S(1)}, u32[]{:S(2)}, u32[]{:S(2)}) collective-permute-start(bf16[2,1,4,3,176,128]{5,4,3,2,0,1:T(8,128)(2,1)S(1)} %get-tuple-element.157), channel_id=1, source_target_pairs={{0,2},{2,0},{4,6},{6,4},{8,10},{10,8},{12,14},{14,12},{16,18},{18,... | collective-permute-start | bytes 3244040 | tf_op jit(solution)/shard_map/ppermute | solution.py:17
  249.5 52.7 %collective-permute-start.6 = (bf16[1,2,4,3,176,128]{5,4,3,2,1,0:T(8,128)(2,1)S(1)}, bf16[1,2,4,3,176,128]{5,4,3,2,1,0:T(8,128)(2,1)S(1)}, u32[]{:S(2)}, u32[]{:S(2)}) collective-permute-start(bf16[1,2,4,3,176,128]{5,4,3,2,1,0:T(8,128)(2,1)S(1)} %get-tuple-element.155), channel_id=1, source_target_pairs={{0,4},{2,6},{4,0},{6,2},{8,12},{10,14},{12,8},{14,10},{16,20},{18,... | collective-permute-start | bytes 3244040 | tf_op jit(solution)/shard_map/ppermute | solution.py:17
  306.4 1.4 copy-start.6
  307.8 1.0 copy-start.10
  309.1 14.3 %collective-permute-start.7 = (bf16[176,1536]{1,0:T(8,128)(2,1)S(1)}, bf16[176,1536]{1,0:T(8,128)(2,1)S(1)}, u32[]{:S(2)}, u32[]{:S(2)}) collective-permute-start(bf16[176,1536]{1,0:T(8,128)(2,1)S(1)} %get-tuple-element.165), channel_id=1, source_target_pairs={{0,2},{2,0},{4,6},{6,4},{8,10},{10,8},{12,14},{14,12},{16,18},{18,... | collective-permute-start | bytes 1622024 | tf_op jit(solution)/shard_map/ppermute | solution.py:17
  323.7 11.2 %copy-start.8 = (bf16[352,1536]{1,0:T(8,128)(2,1)}, bf16[352,1536]{1,0:T(8,128)(2,1)S(1)}, u32[]{:S(2)}) copy-start(bf16[352,1536]{1,0:T(8,128)(2,1)S(1)} %maximum_select_fusion.3) | copy-start | bytes 3244036
  323.7 52.7 %collective-permute-start.8 = (bf16[352,1536]{1,0:T(8,128)(2,1)S(1)}, bf16[352,1536]{1,0:T(8,128)(2,1)}, u32[]{:S(2)}, u32[]{:S(2)}) collective-permute-start(bf16[352,1536]{1,0:T(8,128)(2,1)S(1)} %maximum_select_fusion.3), channel_id=1, source_target_pairs={{0,4},{2,6},{4,0},{6,2},{8,12},{10,14},{12,8},{14,10},{16,20},{18,... | collective-permute-start | bytes 3244040 | tf_op jit(solution)/shard_map/ppermute | solution.py:17
  380.4 4.2 slice-start
  381.3 111.4 %collective-permute-start.9 = (bf16[176,1536]{1,0:T(8,128)(2,1)}, bf16[176,1536]{1,0:T(8,128)(2,1)S(1)}, u32[]{:S(2)}, u32[]{:S(2)}) collective-permute-start(bf16[176,1536]{1,0:T(8,128)(2,1)} %broadcast_select_fusion.2), channel_id=1, source_target_pairs={{0,256},{256,0},{1,257},{257,1},{2,258},{258,2},{3,259},{259,3},{4... | collective-permute-start | bytes 1622024 | tf_op jit(solution)/shard_map/ppermute | solution.py:17
  384.6 109.1 %copy-start.1 = (s32[1,32]{1,0:T(1,128)S(1)}, s32[1,32]{1,0:T(1,128)}, u32[]{:S(2)}) copy-start(s32[1,32]{1,0:T(1,128)} %param.15) | copy-start | bytes 388
  (3 other events, 2.4 us)
where the time goes:
time: 495 us; the launch traced here: 494 us
  waiting for transfers between devices  246 us (50%)
  blocking collectives  105 us (21%)
  local copies, waits for them, and re-layouts  46.1 us (9%)
  starting transfers between devices  44.9 us (9%)
  other arithmetic  33.2 us (7%)
  matrix products  17.4 us (4%)
    ppermute x10, waiting for transfers between devices, swapped(): return lax.ppermute(value, axis, pairs)  246 us
    psum x1, blocking collectives, per_device(): gate_grad = lax.psum(partial_sum, ('grp', 'seq', 'dp'))  105 us
    ppermute x10, starting transfers between devices, swapped(): return lax.ppermute(value, axis, pairs)  44.9 us
  transfers between devices with their start and end apart: 10, of which 8 were waited for; matrix products, arithmetic and copies ran while one was open for 3% of the time, Pallas kernels for 0%

commit v1 on v0

v1 whole, which is shorter than its diff:
```python
import functools
import math

import jax
import jax.numpy as jnp
from jax import lax
from jax.experimental import pallas as pl
from jax.experimental.pallas import tpu as pltpu
from jax.sharding import PartitionSpec as P

HD = 128
GROUP = 4
TXT = 128
SCALE = 1.0 / math.sqrt(HD)
EXP2_SCALE = SCALE * math.log2(math.e)
MESH = pl.DeviceIdType.MESH
BF16 = jnp.bfloat16
F32 = jnp.float32


def flip(index, bit):
    unit = 1 << bit
    return index + unit - 2 * unit * lax.rem(lax.div(index, unit), 2)


def contract(left, right, left_dim, right_dim):
    return lax.dot_general(
        left, right, (((left_dim,), (right_dim,)), ((), ())), preferred_element_type=F32
    )


def kernel(
    heads,
    seq_bits,
    dp_size,
    qkv,
    cot,
    gate,
    tile_map,
    text_count,
    blended,
    grads,
    gate_grad,
    held,
    made,
    back_out,
    back_in,
    res_out,
    res_in,
    perm,
    perm_t,
    sums,
    sums_in,
    shares,
    in_send,
    in_recv,
    out_send,
    out_recv,
    back_sems,
    res_sems,
    sum_send,
    sum_recv,
    share_send,
    share_recv,
):
    core = lax.axis_index("grp")
    position = lax.axis_index("seq")
    member = lax.rem(position, GROUP)
    sequence = lax.div(position, GROUP)
    base = position - member
    rows = qkv.shape[3]
    length = rows * GROUP
    partners = [member, flip(member, 0), flip(member, 1), 3 - member]
    other_core = {"grp": 1 - core}
    steps = [other_core]
    if dp_size == 2:
        steps.append({"dp": 1 - lax.axis_index("dp")})
    steps += [{"seq": flip(position, bit)} for bit in reversed(range(2, seq_bits))]

    def rows_of(which):
        return pl.ds(pl.multiple_of(which * rows, 16), rows)

    def columns_of(which, head):
        return pl.ds(pl.multiple_of((which * heads + head) * HD, HD), HD)

    def in_pair(head, k):
        pairs = []
        theirs = columns_of(partners[k], head)
        mine = rows_of(member)
        for t, (src, dst) in enumerate(
            (
                (qkv.at[0, :, 0, :, theirs], held.at[head, pl.ds(0, 3), mine, :]),
                (cot.at[0, 0, :, theirs], held.at[head, 3, mine, :]),
            )
        ):
            if k == 0:
                pairs.append(pltpu.make_async_copy(src, dst, in_recv.at[head, k, t]))
            else:
                pairs.append(
                    pltpu.make_async_remote_copy(
                        src_ref=src,
                        dst_ref=dst,
                        send_sem=in_send.at[head, k, t],
                        recv_sem=in_recv.at[head, k, t],
                        device_id={"seq": base + partners[k]},
                        device_id_type=MESH,
                    )
                )
        return pairs

    def in_arrival(head, k):
        theirs = rows_of(partners[k])
        pairs = []
        for t, dst in enumerate(
            (held.at[head, pl.ds(0, 3), theirs, :], held.at[head, 3, theirs, :])
        ):
            pairs.append(
                pltpu.make_async_remote_copy(
                    src_ref=dst,
                    dst_ref=dst,
                    send_sem=in_send.at[head, k, t],
                    recv_sem=in_recv.at[head, k, t],
                    device_id={"seq": base + partners[k]},
                    device_id_type=MESH,
                )
            )
        return pairs

    def out_pair(head, k, t):
        theirs = rows_of(partners[k])
        mine = columns_of(member, head)
        if t == 0:
            src, dst = made.at[head, 0, theirs, :], blended.at[0, 0, :, mine]
        else:
            src, dst = made.at[head, pl.ds(1, 3), theirs, :], grads.at[0, :, 0, :, mine]
        if k == 0:
            return pltpu.make_async_copy(src, dst, out_recv.at[head, k, t])
        return pltpu.make_async_remote_copy(
            src_ref=src,
            dst_ref=dst,
            send_sem=out_send.at[head, k, t],
            recv_sem=out_recv.at[head, k, t],
            device_id={"seq": base + partners[k]},
            device_id_type=MESH,
        )

    def out_arrival(head, k, t):
        theirs = columns_of(partners[k], head)
        if t == 0:
            dst = blended.at[0, 0, :, theirs]
        else:
            dst = grads.at[0, :, 0, :, theirs]
        return pltpu.make_async_remote_copy(
            src_ref=dst,
            dst_ref=dst,
            send_sem=out_send.at[head, k, t],
            recv_sem=out_recv.at[head, k, t],
            device_id={"seq": base + partners[k]},
            device_id_type=MESH,
        )

    def back_copy(head):
        return pltpu.make_async_remote_copy(
            src_ref=back_out.at[head],
            dst_ref=back_in.at[head],
            send_sem=back_sems.at[head, 0],
            recv_sem=back_sems.at[head, 1],
            device_id=other_core,
            device_id_type=MESH,
        )

    def res_copy(head):
        return pltpu.make_async_remote_copy(
            src_ref=res_out.at[head],
            dst_ref=res_in.at[head],
            send_sem=res_sems.at[head, 0],
            recv_sem=res_sems.at[head, 1],
            device_id=other_core,
            device_id_type=MESH,
        )

    barrier = pltpu.get_barrier_semaphore()
    peers = [{"seq": base + partners[k]} for k in (1, 2, 3)] + steps
    for peer in peers:
        pl.semaphore_signal(barrier, inc=1, device_id=peer, device_id_type=MESH)
    pl.semaphore_wait(barrier, len(peers))

    for head in range(heads):
        for k in (2, 3, 1, 0):
            for copy in in_pair(head, k):
                copy.start()

    sums[0] = jnp.zeros(sums.shape[1:], F32)

    @pl.when(core == 1)
    def _():
        order = tile_map[0, pl.ds(sequence, 1), :].astype(F32)
        down = lax.broadcasted_iota(jnp.int32, (length, length), 0).astype(F32)
        perm_t[...] = jnp.where(down == order, 1.0, 0.0).astype(BF16)
        order_down = jnp.transpose(jnp.broadcast_to(order, (HD, length)))
        for start in range(0, length, HD):
            width = min(HD, length - start)
            across = lax.broadcasted_iota(jnp.int32, (length, width), 1).astype(F32) + start
            perm[:, start : start + width] = jnp.where(
                order_down[:, :width] == across, 1.0, 0.0
            ).astype(BF16)

    counted = text_count[0, sequence]

    def one_head(head, carry):
        for k in (0, 1, 2, 3):
            for copy in in_pair(head, k) if k == 0 else in_arrival(head, k):
                if k == 0:
                    copy.wait()
                else:
                    copy.wait_recv()

        gains = gate[pl.ds(member * heads + head, 1), :]

        @pl.when(core == 1)
        def _():
            back_out[head] = contract(perm[...], held[head, 3], 1, 0).astype(BF16)
            back_copy(head).start()

        @pl.when(core == 0)
        def _():
            back_copy(head).wait_recv()
            held[head, 3] = (
                held[head, 3].astype(F32) + gains * back_in[head].astype(F32)
            ).astype(BF16)

        keys = held[head, 1]
        values = held[head, 2]
        key_sum = None
        for start in range(0, length, 256):
            width = min(256, length - start)
            span = pl.ds(start, width)
            queries = held[head, 0, span, :]
            grad = held[head, 3, span, :]
            scores = contract(keys, queries, 1, 1)
            text = lax.broadcasted_iota(jnp.int32, (TXT, width), 0) < counted
            scores = jnp.concatenate(
                [jnp.where(text, scores[:TXT], -jnp.inf), scores[TXT:]], axis=0
            )
            top = jnp.max(scores, axis=0, keepdims=True)
            grown = jnp.exp2((scores - top) * EXP2_SCALE)
            probs = grown * (1.0 / jnp.sum(grown, axis=0, keepdims=True))
            probs_low = probs.astype(BF16)
            made[head, 0, span, :] = jnp.transpose(contract(values, probs_low, 0, 0)).astype(BF16)
            grad_probs = contract(values, grad, 1, 1)
            centre = jnp.sum(probs * grad_probs, axis=0, keepdims=True)
            shifted = (probs * (grad_probs - centre)).astype(BF16)
            made[head, 1, span, :] = (
                jnp.transpose(contract(keys, shifted, 0, 0)) * SCALE
            ).astype(BF16)
            key_part = contract(shifted, queries, 1, 0)
            value_part = contract(probs_low, grad, 1, 0)
            key_sum = key_part if key_sum is None else key_sum + key_part
            value_sum = value_part if start == 0 else value_sum + value_part
        made[head, 2] = (key_sum * SCALE).astype(BF16)
        made[head, 3] = value_sum.astype(BF16)
        for k in (2, 3, 1, 0):
            out_pair(head, k, 1).start()

        @pl.when(core == 0)
        def _():
            own = made[head, 0].astype(F32)
            res_out[head] = (gains * own).astype(BF16)
            res_copy(head).start()
            sums[0, pl.ds(head, 1), :] = jnp.sum(
                own * back_in[head].astype(F32), axis=0, keepdims=True
            )

        @pl.when(core == 1)
        def _():
            res_copy(head).wait_recv()
            placed = contract(perm_t[...], res_in[head], 1, 0)
            made[head, 0] = (made[head, 0].astype(F32) + placed).astype(BF16)

        for k in (2, 3, 1, 0):
            out_pair(head, k, 0).start()
        return carry

    lax.fori_loop(0, heads, one_head, 0)

    for step, peer in enumerate(steps):
        copy = pltpu.make_async_remote_copy(
            src_ref=sums.at[step],
            dst_ref=sums_in.at[step],
            send_sem=sum_send.at[step],
            recv_sem=sum_recv.at[step],
            device_id=peer,
            device_id_type=MESH,
        )
        copy.start()
        copy.wait()
        sums[step + 1] = sums[step] + sums_in[step]
    last = sums.at[len(steps)]

    def share_copy(k, slot):
        return pltpu.make_async_remote_copy(
            src_ref=last,
            dst_ref=shares.at[slot],
            send_sem=share_send.at[k],
            recv_sem=share_recv.at[k],
            device_id={"seq": base + partners[k]},
            device_id_type=MESH,
        )

    for k in (2, 3, 1):
        share_copy(k, member).start()
    shares[member] = last[...]
    for k in (1, 2, 3):
        share_copy(k, partners[k]).wait_recv()
    for k in (1, 2, 3):
        share_copy(k, member).wait_send()
    for which in range(GROUP):
        gate_grad[which * heads : (which + 1) * heads, :] = shares[which, :heads, :]

    def finish(head, carry):
        for k in (1, 2, 3):
            for copy in in_pair(head, k):
                copy.wait_send()
        for t in (0, 1):
            out_pair(head, 0, t).wait()
            for k in (1, 2, 3):
                out_pair(head, k, t).wait_send()
                out_arrival(head, k, t).wait_recv()

        @pl.when(core == 0)
        def _():
            res_copy(head).wait_send()

        @pl.when(core == 1)
        def _():
            back_copy(head).wait_send()

        return carry

    lax.fori_loop(0, heads, finish, 0)


def per_device(mesh, qkv, cotangent, gate, tile_map, text_count):
    rows, channels = qkv.shape[3:]
    length = rows * GROUP
    heads = channels // HD // GROUP
    seq_bits = mesh.shape["seq"].bit_length() - 1
    dp_size = mesh.shape["dp"]
    step_count = 1 + (dp_size == 2) + seq_bits - 2
    vmem = pl.BlockSpec(memory_space=pltpu.VMEM)
    any_space = pl.BlockSpec(memory_space=pl.ANY)
    dma = pltpu.SemaphoreType.DMA
    blended, grads, gate_grad = pl.pallas_call(
        functools.partial(kernel, heads, seq_bits, dp_size),
        out_shape=(
            jax.ShapeDtypeStruct(cotangent.shape, BF16),
            jax.ShapeDtypeStruct(qkv.shape, BF16),
            jax.ShapeDtypeStruct((channels // HD, HD), F32),
        ),
        in_specs=[
            any_space,
            any_space,
            vmem,
            vmem,
            pl.BlockSpec(memory_space=pltpu.SMEM),
        ],
        out_specs=(any_space, any_space, vmem),
        scratch_shapes=[
            pltpu.VMEM((heads, 4, length, HD), BF16),
            pltpu.VMEM((heads, 4, length, HD), BF16),
            pltpu.VMEM((heads, length, HD), BF16),
            pltpu.VMEM((heads, length, HD), BF16),
            pltpu.VMEM((heads, length, HD), BF16),
            pltpu.VMEM((heads, length, HD), BF16),
            pltpu.VMEM((length, length), BF16),
            pltpu.VMEM((length, length), BF16),
            pltpu.VMEM((step_count + 1, 8, HD), F32),
            pltpu.VMEM((step_count, 8, HD), F32),
            pltpu.VMEM((GROUP, 8, HD), F32),
            dma((heads, GROUP, 2)),
            dma((heads, GROUP, 2)),
            dma((heads, GROUP, 2)),
            dma((heads, GROUP, 2)),
            dma((heads, 2)),
            dma((heads, 2)),
            dma((step_count,)),
            dma((step_count,)),
            dma((GROUP,)),
            dma((GROUP,)),
        ],
        compiler_params=pltpu.CompilerParams(
            collective_id=0, has_side_effects=True, vmem_limit_bytes=48 * 1024 * 1024
        ),
    )(qkv, cotangent, gate.reshape(channels // HD, HD), tile_map, text_count)
    return blended, grads, gate_grad.reshape(channels)


def solution(mesh):
    placed = (
        P("grp", None, "dp", "seq", None),
        P("grp", "dp", "seq", None),
        P(),
        P("dp", None, None),
        P("dp", None),
    )
    return jax.shard_map(
        functools.partial(per_device, mesh),
        mesh=mesh,
        in_specs=placed,
        out_specs=(P("grp", "dp", "seq", None), P("grp", None, "dp", "seq", None), P()),
        check_vma=False,
    )
```

time: 495 us -> 121 us (0.24)
  the two profiles are of different devices: /device:TPU:1 before, /device:TPU:2 now
where the time goes in v1:
time: 121 us; the launch traced here: 120 us
  Pallas kernels  112 us (93%)
  local copies, waits for them, and re-layouts  7.27 us (6%)
    pallas_call x1, Pallas kernels, per_device(): pl.pallas_call(functools.partial(kernel, heads, seq_bits, dp_size), out_s...  112 us
    unnamed x13, local copies, waits for them, and re-layouts  7.27 us

profile of v1, /device:TPU:2, one launch (start us, length us, event | category | flops | bytes accessed | tf_op | source)
XLA Modules:
  0.0 120.3 jit_solution(5354643065408309723)
XLA Ops:
  0.6 0.0 copy-start
  0.6 1.4 %copy-done = bf16[1,3,1,176,1536]{4,3,2,1,0:T(8,128)(2,1)S(1)} copy-done((bf16[1,3,1,176,1536]{4,3,2,1,0:T(8,128)(2,1)S(1)}, bf16[1,3,1,176,1536]{4,3,2,1,0:T(8,128)(2,1)}, u32[]{:S(2)}) %copy-start) | copy-done | bytes 1622040
  2.1 0.0 copy-start.1
  2.1 1.0 copy-done.1
  3.1 0.0 copy-start.2
  3.1 0.9 copy-done.2
  4.0 0.0 copy-start.3
  4.0 0.7 copy-done.3
  4.7 0.0 copy-start.4
  4.7 0.7 copy-done.4
  5.4 112.4 %shard_map.76 = (bf16[1,1,176,1536]{3,2,1,0:T(8,128)(2,1)S(1)}, bf16[1,3,1,176,1536]{4,3,2,1,0:T(8,128)(2,1)S(1)}, f32[12,128]{1,0:T(8,128)S(1)}) custom-call(bf16[1,3,1,176,1536]{4,3,2,1,0:T(8,128)(2,1)S(1)} %copy-done, bf16[1,1,176,1536]{3,2,1,0:T(8,128)(2,1)S(1)} %copy-done.1, f32[12,128]{1,0:T(8,128)S(1)} %bitcast.2, s32[1,32,704]{2,1,0:T(8,128)S(1)} %copy-done.2, ...), custom_call_target="tpu_custom_call" | custom-call | tf_op jit(solution)/shard_map/pallas_call | solution.py:353
  117.8 0.8 copy.11
  118.6 1.2 copy.12
  119.7 0.6 copy.13
Async XLA Ops:
  0.6 1.4 %copy-start = (bf16[1,3,1,176,1536]{4,3,2,1,0:T(8,128)(2,1)S(1)}, bf16[1,3,1,176,1536]{4,3,2,1,0:T(8,128)(2,1)}, u32[]{:S(2)}) copy-start(bf16[1,3,1,176,1536]{4,3,2,1,0:T(8,128)(2,1)} %qkv.1) | copy-start | bytes 4866052
  2.1 1.0 copy-start.1
  3.1 0.9 copy-start.2
  4.0 0.7 copy-start.3
  4.7 0.7 copy-start.4

commit v2 on v1

v2 whole, which is shorter than its diff:
```python
import functools
import math

import jax
import jax.numpy as jnp
from jax import lax
from jax.experimental import pallas as pl
from jax.experimental.pallas import tpu as pltpu
from jax.sharding import PartitionSpec as P

HD = 128
GROUP = 4
TXT = 128
BLOCK = 704
SCALE = 1.0 / math.sqrt(HD)
EXP2_SCALE = SCALE * math.log2(math.e)
MESH = pl.DeviceIdType.MESH
BF16 = jnp.bfloat16
F32 = jnp.float32


def flip(index, bit):
    unit = 1 << bit
    return index + unit - 2 * unit * lax.rem(lax.div(index, unit), 2)


def contract(left, right, left_dim, right_dim):
    return lax.dot_general(
        left, right, (((left_dim,), (right_dim,)), ((), ())), preferred_element_type=F32
    )


def kernel(
    heads,
    sizes,
    qkv,
    cot,
    gate,
    tile_map,
    text_count,
    blended,
    grads,
    gate_grad,
    held,
    made,
    back_out,
    back_in,
    res_out,
    res_in,
    perm,
    perm_t,
    probs_all,
    probs_low_all,
    order_all,
    gains_all,
    counts,
    partial,
    z_slots,
    x_slots,
    y_slots,
    total,
    in_send,
    in_recv,
    out_send,
    out_recv,
    back_sems,
    res_sems,
    round_send,
    round_recv,
    total_sems,
    small_sems,
):
    z_size, dp_size, x_size, y_size = sizes
    core = lax.axis_index("grp")
    position = lax.axis_index("seq")
    sample = lax.axis_index("dp")
    member = lax.rem(position, GROUP)
    sequence = lax.div(position, GROUP)
    base = position - member
    rows = qkv.shape[3]
    length = rows * GROUP
    partners = [member, flip(member, 0), flip(member, 1), 3 - member]
    other_core = {"grp": 1 - core}

    y_place = lax.rem(sequence, y_size)
    ring_place = y_place * GROUP + member
    ring_base = position - ring_place
    x_place = lax.rem(lax.div(sequence, y_size), x_size)
    z_high = lax.div(sequence, y_size * x_size)
    z_place = z_high * dp_size + sample
    z_stride = GROUP * y_size * x_size
    rounds = [
        (
            z_place,
            z_size * dp_size,
            z_slots,
            lambda p: {
                "seq": position + (lax.div(p, dp_size) - z_high) * z_stride,
                "dp": lax.rem(p, dp_size),
            },
        ),
        (
            x_place,
            x_size,
            x_slots,
            lambda p: {"seq": position + (p - x_place) * GROUP * y_size},
        ),
        (ring_place, GROUP * y_size, y_slots, lambda p: {"seq": ring_base + p}),
    ]

    def rows_of(which):
        return pl.ds(pl.multiple_of(which * rows, 16), rows)

    def columns_of(which, head):
        return pl.ds(pl.multiple_of((which * heads + head) * HD, HD), HD)

    def remote(src, dst, send_sem, recv_sem, device):
        return pltpu.make_async_remote_copy(
            src_ref=src,
            dst_ref=dst,
            send_sem=send_sem,
            recv_sem=recv_sem,
            device_id=device,
            device_id_type=MESH,
        )

    def in_pair(head, k):
        theirs = columns_of(partners[k], head)
        mine = rows_of(member)
        ends = (
            (qkv.at[0, :, 0, :, theirs], held.at[head, pl.ds(0, 3), mine, :]),
            (cot.at[0, 0, :, theirs], held.at[head, 3, mine, :]),
        )
        if k == 0:
            return [
                pltpu.make_async_copy(src, dst, in_recv.at[head, k, t])
                for t, (src, dst) in enumerate(ends)
            ]
        return [
            remote(
                src,
                dst,
                in_send.at[head, k, t],
                in_recv.at[head, k, t],
                {"seq": base + partners[k]},
            )
            for t, (src, dst) in enumerate(ends)
        ]

    def in_arrival(head, k):
        theirs = rows_of(partners[k])
        return [
            remote(
                dst,
                dst,
                in_send.at[head, k, t],
                in_recv.at[head, k, t],
                {"seq": base + partners[k]},
            )
            for t, dst in enumerate(
                (held.at[head, pl.ds(0, 3), theirs, :], held.at[head, 3, theirs, :])
            )
        ]

    def out_pair(head, k, t):
        theirs = rows_of(partners[k])
        mine = columns_of(member, head)
        if t == 0:
            src, dst = made.at[head, 0, theirs, :], blended.at[0, 0, :, mine]
        else:
            src, dst = made.at[head, pl.ds(1, 3), theirs, :], grads.at[0, :, 0, :, mine]
        if k == 0:
            return pltpu.make_async_copy(src, dst, out_recv.at[head, k, t])
        return remote(
            src,
            dst,
            out_send.at[head, k, t],
            out_recv.at[head, k, t],
            {"seq": base + partners[k]},
        )

    def out_arrival(head, k, t):
        theirs = columns_of(partners[k], head)
        dst = blended.at[0, 0, :, theirs] if t == 0 else grads.at[0, :, 0, :, theirs]
        return remote(
            dst,
            dst,
            out_send.at[head, k, t],
            out_recv.at[head, k, t],
            {"seq": base + partners[k]},
        )

    def back_copy(head):
        return remote(
            back_out.at[head],
            back_in.at[head],
            back_sems.at[head, 0],
            back_sems.at[head, 1],
            other_core,
        )

    def res_copy(head):
        return remote(
            res_out.at[head],
            res_in.at[head],
            res_sems.at[head, 0],
            res_sems.at[head, 1],
            other_core,
        )

    total_copy = remote(total, total, total_sems.at[0], total_sems.at[1], other_core)

    def round_copies(which):
        place, number, slots, device = rounds[which]
        return [
            remote(
                slots.at[place],
                slots.at[place],
                round_send.at[which, ahead],
                round_recv.at[which, ahead],
                device(lax.rem(place + ahead, number)),
            )
            for ahead in range(1, number)
        ]

    def round_start(which, mine):
        place, _, slots, _ = rounds[which]
        slots[place] = mine
        for copy in round_copies(which):
            copy.start()

    def round_finish(which):
        place, number, slots, device = rounds[which]
        for ahead in range(1, number):
            sender = lax.rem(place + number - ahead, number)
            remote(
                slots.at[sender],
                slots.at[sender],
                round_send.at[which, ahead],
                round_recv.at[which, ahead],
                device(sender),
            ).wait_recv()
        for copy in round_copies(which):
            copy.wait_send()

    def slot_sum(which):
        _, number, slots, _ = rounds[which]
        added = slots[0]
        for slot in range(1, number):
            added = added + slots[slot]
        return added

    small = [
        pltpu.make_async_copy(src, dst, small_sems.at[i])
        for i, (src, dst) in enumerate(
            ((tile_map, order_all), (gate, gains_all), (text_count, counts))
        )
    ]
    for copy in small:
        copy.start()
    for head in range(heads):
        for copy in in_pair(head, 0):
            copy.start()

    barrier = pltpu.get_barrier_semaphore()
    near = [{"seq": base + partners[k]} for k in (1, 2, 3)] + [other_core]
    for peer in near:
        pl.semaphore_signal(barrier, inc=1, device_id=peer, device_id_type=MESH)

    @pl.when(core == 0)
    def _():
        far = []
        for place, number, _, device in rounds[:2]:
            far += [device(lax.rem(place + ahead, number)) for ahead in range(1, number)]
        if y_size == 2:
            far += [{"seq": ring_base + (1 - y_place) * GROUP + k} for k in range(GROUP)]
        for peer in far:
            pl.semaphore_signal(barrier, inc=1, device_id=peer, device_id_type=MESH)
        pl.semaphore_wait(barrier, len(near) + len(far))

    @pl.when(core == 1)
    def _():
        pl.semaphore_wait(barrier, len(near))

    for head in range(heads - 1):
        for k in (2, 3, 1):
            for copy in in_pair(head, k):
                copy.start()

    for copy in small:
        copy.wait()
    partial[...] = jnp.zeros(partial.shape, F32)
    counted = counts[0, sequence]

    @pl.when(core == 1)
    def _():
        order = order_all[0, pl.ds(sequence, 1), :].astype(F32)
        down = lax.broadcasted_iota(jnp.int32, (length, length), 0).astype(F32)
        perm_t[...] = jnp.where(down == order, 1.0, 0.0).astype(BF16)
        order_down = jnp.transpose(jnp.broadcast_to(order, (HD, length)))
        for start in range(0, length, HD):
            width = min(HD, length - start)
            across = lax.broadcasted_iota(jnp.int32, (length, width), 1).astype(F32) + start
            perm[:, start : start + width] = jnp.where(
                order_down[:, :width] == across, 1.0, 0.0
            ).astype(BF16)

    for k in (2, 3, 1):
        for copy in in_pair(0, k):
            copy.wait_send()
    for k in (2, 3, 1):
        for copy in in_pair(heads - 1, k):
            copy.start()

    def arrive(head):
        for k in range(GROUP):
            for copy in in_pair(head, k) if k == 0 else in_arrival(head, k):
                if k == 0:
                    copy.wait()
                else:
                    copy.wait_recv()

        @pl.when(core == 1)
        def _():
            back_out[head] = contract(perm[...], held[head, 3], 1, 0).astype(BF16)
            back_copy(head).start()

    def depart(head):
        for k in (2, 3, 1, 0):
            out_pair(head, k, 1).start()

        @pl.when(core == 1)
        def _():
            res_copy(head).wait_recv()
            placed = contract(perm_t[...], res_in[head], 1, 0)
            made[head, 0] = (made[head, 0].astype(F32) + placed).astype(BF16)

        for k in (2, 3, 1, 0):
            out_pair(head, k, 0).start()

    for head in range(heads - 1):
        arrive(head)

    blocks = [(start, min(BLOCK, length - start)) for start in range(0, length, BLOCK)]

    def one_head(head, carry):
        @pl.when(head == heads - 1)
        def _():
            arrive(head)

        gains = gains_all[pl.ds(member * heads + head, 1), :]
        keys = held[head, 1]
        values = held[head, 2]
        for start, width in blocks:
            span = pl.ds(start, width)
            scores = contract(keys, held[head, 0, span, :], 1, 1)
            text = lax.broadcasted_iota(jnp.int32, (TXT, width), 0) < counted
            scores = jnp.concatenate(
                [jnp.where(text, scores[:TXT], -jnp.inf), scores[TXT:]], axis=0
            )
            top = jnp.max(scores, axis=0, keepdims=True)
            grown = jnp.exp2((scores - top) * EXP2_SCALE)
            probs = grown * (1.0 / jnp.sum(grown, axis=0, keepdims=True))
            probs_low = probs.astype(BF16)
            probs_all[:, start : start + width] = probs
            probs_low_all[:, start : start + width] = probs_low
            made[head, 0, span, :] = jnp.transpose(contract(values, probs_low, 0, 0)).astype(BF16)

        @pl.when(core == 0)
        def _():
            own = made[head, 0].astype(F32)
            res_out[head] = (gains * own).astype(BF16)
            res_copy(head).start()
            back_copy(head).wait_recv()
            back = back_in[head].astype(F32)
            partial[pl.ds(head, 1), :] = jnp.sum(own * back, axis=0, keepdims=True)
            held[head, 3] = (held[head, 3].astype(F32) + gains * back).astype(BF16)

            @pl.when(head == heads - 1)
            def _():
                round_start(0, partial[...])
                round_finish(0)
                round_start(1, slot_sum(0))
                round_finish(1)
                round_start(2, slot_sum(1))

        key_sum = value_sum = None
        for start, width in blocks:
            span = pl.ds(start, width)
            queries = held[head, 0, span, :]
            grad = held[head, 3, span, :]
            probs = probs_all[:, start : start + width]
            grad_probs = contract(values, grad, 1, 1)
            centre = jnp.sum(probs * grad_probs, axis=0, keepdims=True)
            shifted = (probs * (grad_probs - centre)).astype(BF16)
            made[head, 1, span, :] = (
                jnp.transpose(contract(keys, shifted, 0, 0)) * SCALE
            ).astype(BF16)
            key_part = contract(shifted, queries, 1, 0)
            value_part = contract(probs_low_all[:, start : start + width], grad, 1, 0)
            key_sum = key_part if key_sum is None else key_sum + key_part
            value_sum = value_part if value_sum is None else value_sum + value_part
        made[head, 2] = (key_sum * SCALE).astype(BF16)
        made[head, 3] = value_sum.astype(BF16)

        @pl.when(head == heads - 2)
        def _():
            for later in range(1, heads):
                for k in (2, 3, 1):
                    for copy in in_pair(later, k):
                        copy.wait_send()
            for earlier in range(heads - 1):
                depart(earlier)

        @pl.when(head == heads - 1)
        def _():
            depart(head)

        return carry

    lax.fori_loop(0, heads, one_head, 0)

    @pl.when(core == 0)
    def _():
        round_finish(2)
        for which in range(GROUP):
            added = y_slots[which, :heads, :]
            for half in range(1, y_size):
                added = added + y_slots[half * GROUP + which, :heads, :]
            total[which * heads : (which + 1) * heads, :] = added
        total_copy.start()
        total_copy.wait_send()

    @pl.when(core == 1)
    def _():
        total_copy.wait_recv()

    gate_grad[...] = total[...]

    def finish(head, carry):
        for t in (0, 1):
            out_pair(head, 0, t).wait()
            for k in (1, 2, 3):
                out_pair(head, k, t).wait_send()
                out_arrival(head, k, t).wait_recv()

        @pl.when(core == 0)
        def _():
            res_copy(head).wait_send()

        @pl.when(core == 1)
        def _():
            back_copy(head).wait_send()

        return carry

    lax.fori_loop(0, heads, finish, 0)


def per_device(mesh, qkv, cotangent, gate, tile_map, text_count):
    rows, channels = qkv.shape[3:]
    length = rows * GROUP
    heads = channels // HD // GROUP
    groups = mesh.shape["seq"] // GROUP
    dp_size = mesh.shape["dp"]
    y_size = min(2, groups)
    x_size = min(4, groups // y_size)
    z_size = groups // (y_size * x_size)
    places = max(z_size * dp_size, x_size, GROUP * y_size)
    vmem = pl.BlockSpec(memory_space=pltpu.VMEM)
    hbm = pl.BlockSpec(memory_space=pltpu.HBM)
    any_space = pl.BlockSpec(memory_space=pl.ANY)
    dma = pltpu.SemaphoreType.DMA
    blended, grads, gate_grad = pl.pallas_call(
        functools.partial(kernel, heads, (z_size, dp_size, x_size, y_size)),
        out_shape=(
            jax.ShapeDtypeStruct(cotangent.shape, BF16),
            jax.ShapeDtypeStruct(qkv.shape, BF16),
            jax.ShapeDtypeStruct((channels // HD, HD), F32),
        ),
        in_specs=[hbm] * 5,
        out_specs=(any_space, any_space, vmem),
        scratch_shapes=[
            pltpu.VMEM((heads, 4, length, HD), BF16),
            pltpu.VMEM((heads, 4, length, HD), BF16),
            pltpu.VMEM((heads, length, HD), BF16),
            pltpu.VMEM((heads, length, HD), BF16),
            pltpu.VMEM((heads, length, HD), BF16),
            pltpu.VMEM((heads, length, HD), BF16),
            pltpu.VMEM((length, length), BF16),
            pltpu.VMEM((length, length), BF16),
            pltpu.VMEM((length, length), F32),
            pltpu.VMEM((length, length), BF16),
            pltpu.VMEM(tile_map.shape, jnp.int32),
            pltpu.VMEM((channels // HD, HD), F32),
            pltpu.SMEM(text_count.shape, jnp.int32),
            pltpu.VMEM((8, HD), F32),
            pltpu.VMEM((z_size * dp_size, 8, HD), F32),
            pltpu.VMEM((x_size, 8, HD), F32),
            pltpu.VMEM((GROUP * y_size, 8, HD), F32),
            pltpu.VMEM((channels // HD, HD), F32),
            dma((heads, GROUP, 2)),
            dma((heads, GROUP, 2)),
            dma((heads, GROUP, 2)),
            dma((heads, GROUP, 2)),
            dma((heads, 2)),
            dma((heads, 2)),
            dma((3, places)),
            dma((3, places)),
            dma((2,)),
            dma((3,)),
        ],
        compiler_params=pltpu.CompilerParams(
            collective_id=0, has_side_effects=True, vmem_limit_bytes=60 * 1024 * 1024
        ),
    )(qkv, cotangent, gate.reshape(channels // HD, HD), tile_map, text_count)
    return blended, grads, gate_grad.reshape(channels)


def solution(mesh):
    placed = (
        P("grp", None, "dp", "seq", None),
        P("grp", "dp", "seq", None),
        P(),
        P("dp", None, None),
        P("dp", None),
    )
    return jax.shard_map(
        functools.partial(per_device, mesh),
        mesh=mesh,
        in_specs=placed,
        out_specs=(P("grp", "dp", "seq", None), P("grp", None, "dp", "seq", None), P()),
        check_vma=False,
    )
```

time: 121 us -> 106 us (0.88)
  the two profiles are of different devices: /device:TPU:2 before, /device:TPU:1 now
where the time goes in v2:
time: 106 us; the launch traced here: 105 us
  Pallas kernels  99.5 us (94%)
  local copies, waits for them, and re-layouts  5.18 us (5%)
    pallas_call x1, Pallas kernels, per_device(): pl.pallas_call(functools.partial(kernel, heads, (z_size, dp_size, x_size,...  99.5 us
    unnamed x5, local copies, waits for them, and re-layouts  5.18 us

profile of v2, /device:TPU:1, one launch (start us, length us, event | category | flops | bytes accessed | tf_op | source)
XLA Modules:
  0.0 105.3 jit_solution(10945522446053523151)
XLA Ops:
  0.6 99.5 %shard_map.76 = (bf16[1,1,176,1536]{3,2,1,0:T(8,128)(2,1)}, bf16[1,3,1,176,1536]{4,3,2,1,0:T(8,128)(2,1)}, f32[12,128]{1,0:T(8,128)}) custom-call(bf16[1,3,1,176,1536]{4,3,2,1,0:T(8,128)(2,1)} %qkv.1, bf16[1,1,176,1536]{3,2,1,0:T(8,128)(2,1)} %cot.1, f32[12,128]{1,0:T(8,128)} %bitcast.2, s32[1,32,704]{2,1,0:T(8,128)} %tile_map.1, s32[1,32]{1,0:T(1,128)} %text_count.1), custom_call_target="tpu_custom_call" | custom-call | tf_op jit(solution)/shard_map/pallas_call | solution.py:474
  100.1 1.9 %copy.11 = bf16[1,1,176,1536]{3,2,1,0:T(8,128)(2,1)} copy(bf16[1,1,176,1536]{3,2,1,0:T(8,128)(2,1)} %get-tuple-element.12) | data formatting | bytes 1081344
  102.0 0.0 copy-start
  102.0 2.7 %copy.12 = bf16[1,3,1,176,1536]{4,3,2,1,0:T(8,128)(2,1)} copy(bf16[1,3,1,176,1536]{4,3,2,1,0:T(8,128)(2,1)} %get-tuple-element.13) | data formatting | bytes 3244032
  104.7 0.0 copy-done
  104.7 0.6 copy.13
Async XLA Ops:
  102.0 2.7 %copy-start = (f32[12,128]{1,0:T(8,128)S(1)}, f32[12,128]{1,0:T(8,128)}, u32[]{:S(2)}) copy-start(f32[12,128]{1,0:T(8,128)} %get-tuple-element.8) | copy-start | bytes 18436

commit v3 on v2

--- a/solution.py
+++ b/solution.py
@@ -457,6 +457,18 @@
     lax.fori_loop(0, heads, finish, 0)
 
 
+def store(*refs):
+    sems = refs[-1]
+    number = len(refs) // 2
+    copies = [
+        pltpu.make_async_copy(refs[i], refs[number + i], sems.at[i]) for i in range(number)
+    ]
+    for copy in copies:
+        copy.start()
+    for copy in copies:
+        copy.wait()
+
+
 def per_device(mesh, qkv, cotangent, gate, tile_map, text_count):
     rows, channels = qkv.shape[3:]
     length = rows * GROUP
@@ -474,9 +486,9 @@
     blended, grads, gate_grad = pl.pallas_call(
         functools.partial(kernel, heads, (z_size, dp_size, x_size, y_size)),
         out_shape=(
-            jax.ShapeDtypeStruct(cotangent.shape, BF16),
-            jax.ShapeDtypeStruct(qkv.shape, BF16),
-            jax.ShapeDtypeStruct((channels // HD, HD), F32),
+            pltpu.VMEM(cotangent.shape, BF16),
+            pltpu.VMEM(qkv.shape, BF16),
+            pltpu.VMEM((channels // HD, HD), F32),
         ),
         in_specs=[hbm] * 5,
         out_specs=(any_space, any_space, vmem),
@@ -511,10 +523,22 @@
             dma((3,)),
         ],
         compiler_params=pltpu.CompilerParams(
-            collective_id=0, has_side_effects=True, vmem_limit_bytes=60 * 1024 * 1024
+            collective_id=0, has_side_effects=True, vmem_limit_bytes=44 * 1024 * 1024
         ),
-    )(qkv, cotangent, gate.reshape(channels // HD, HD), tile_map, text_count)
-    return blended, grads, gate_grad.reshape(channels)
+    )(
+        *(
+            pltpu.with_memory_space_constraint(operand, pltpu.HBM)
+            for operand in (qkv, cotangent, gate.reshape(channels // HD, HD), tile_map, text_count)
+        )
+    )
+    results = (blended, grads, gate_grad.reshape(channels))
+    return pl.pallas_call(
+        store,
+        out_shape=tuple(pltpu.HBM(result.shape, result.dtype) for result in results),
+        in_specs=[any_space] * 3,
+        out_specs=(any_space,) * 3,
+        scratch_shapes=[dma((3,))],
+    )(*(pltpu.with_memory_space_constraint(result, pltpu.VMEM) for result in results))
 
 
 def solution(mesh):

time: 106 us -> 102 us (0.962)
  local copies, waits for them, and re-layouts: 5.18 us -> 0 us
    unnamed x5 -> x0, local copies, waits for them, and re-layouts: 5.18 us -> none
    pallas_call x0 -> x1, Pallas kernels: none -> 1.37 us  [per_device(): pl.pallas_call(store, out_shape=tuple((pltpu.HBM(result.shape, result.dty...]
where the time goes in v3:
time: 102 us; the launch traced here: 101 us
  Pallas kernels  100 us (98%)
    pallas_call x1, Pallas kernels, per_device(): pl.pallas_call(functools.partial(kernel, heads, (z_size, dp_size, x_size,...  98.9 us

profile of v3, /device:TPU:1, one launch (start us, length us, event | category | flops | bytes accessed | tf_op | source)
XLA Modules:
  0.0 100.9 jit_solution(1497500063318954742)
XLA Ops:
  0.6 98.9 %shard_map.76 = (bf16[1,1,176,1536]{3,2,1,0:T(8,128)(2,1)S(1)}, bf16[1,3,1,176,1536]{4,3,2,1,0:T(8,128)(2,1)S(1)}, f32[12,128]{1,0:T(8,128)S(1)}) custom-call(bf16[1,3,1,176,1536]{4,3,2,1,0:T(8,128)(2,1)} %qkv.1, bf16[1,1,176,1536]{3,2,1,0:T(8,128)(2,1)} %cot.1, f32[12,128]{1,0:T(8,128)} %bitcast.3, s32[1,32,704]{2,1,0:T(8,128)} %tile_map.1, s32[1,32]{1,0:T(1,128)} %text_count.1), custom_call_target="tpu_custom_call" | custom-call | tf_op jit(solution)/shard_map/pallas_call | solution.py:486
  99.5 1.4 %shard_map.77 = (bf16[1,1,176,1536]{3,2,1,0:T(8,128)(2,1)}, bf16[1,3,1,176,1536]{4,3,2,1,0:T(8,128)(2,1)}, f32[1536]{0:T(1024)}) custom-call(bf16[1,1,176,1536]{3,2,1,0:T(8,128)(2,1)S(1)} %get-tuple-element.6.refs_0_, bf16[1,3,1,176,1536]{4,3,2,1,0:T(8,128)(2,1)S(1)} %get-tuple-element.7.refs_1_, f32[1536]{0:T(1024)S(1)} %bitcast.2), custom_call_target="tpu_custom_call" | custom-call | tf_op jit(solution)/shard_map/pallas_call | solution.py:535

commit v4 on v3

--- a/solution.py
+++ b/solution.py
@@ -379,10 +379,6 @@
             @pl.when(head == heads - 1)
             def _():
                 round_start(0, partial[...])
-                round_finish(0)
-                round_start(1, slot_sum(0))
-                round_finish(1)
-                round_start(2, slot_sum(1))
 
         key_sum = value_sum = None
         for start, width in blocks:
@@ -403,18 +399,14 @@
         made[head, 2] = (key_sum * SCALE).astype(BF16)
         made[head, 3] = value_sum.astype(BF16)
 
-        @pl.when(head == heads - 2)
-        def _():
-            for later in range(1, heads):
-                for k in (2, 3, 1):
-                    for copy in in_pair(later, k):
-                        copy.wait_send()
-            for earlier in range(heads - 1):
-                depart(earlier)
-
-        @pl.when(head == heads - 1)
-        def _():
-            depart(head)
+        @pl.when((core == 0) & (head == heads - 1))
+        def _():
+            round_finish(0)
+            round_start(1, slot_sum(0))
+            round_finish(1)
+            round_start(2, slot_sum(1))
+
+        depart(head)
 
         return carry
 
@@ -438,6 +430,12 @@
     gate_grad[...] = total[...]
 
     def finish(head, carry):
+        @pl.when(head > 0)
+        def _():
+            for k in (1, 2, 3):
+                for copy in in_pair(head, k):
+                    copy.wait_send()
+
         for t in (0, 1):
             out_pair(head, 0, t).wait()
             for k in (1, 2, 3):

time: 102 us -> 102 us (level)
  no operation moved by 1% of the time
where the time goes in v4:
time: 102 us
  Pallas kernels  101 us (99%)
    pallas_call x1, Pallas kernels, per_device(): pl.pallas_call(functools.partial(kernel, heads, (z_size, dp_size, x_size,...  99.6 us

profile of v4, /device:TPU:1, one launch (start us, length us, event | category | flops | bytes accessed | tf_op | source)
XLA Modules:
  0.0 101.6 jit_solution(17186348734146845455)
XLA Ops:
  0.6 99.6 %shard_map.76 = (bf16[1,1,176,1536]{3,2,1,0:T(8,128)(2,1)S(1)}, bf16[1,3,1,176,1536]{4,3,2,1,0:T(8,128)(2,1)S(1)}, f32[12,128]{1,0:T(8,128)S(1)}) custom-call(bf16[1,3,1,176,1536]{4,3,2,1,0:T(8,128)(2,1)} %qkv.1, bf16[1,1,176,1536]{3,2,1,0:T(8,128)(2,1)} %cot.1, f32[12,128]{1,0:T(8,128)} %bitcast.3, s32[1,32,704]{2,1,0:T(8,128)} %tile_map.1, s32[1,32]{1,0:T(1,128)} %text_count.1), custom_call_target="tpu_custom_call" | custom-call | tf_op jit(solution)/shard_map/pallas_call | solution.py:484
  100.2 1.4 %shard_map.77 = (bf16[1,1,176,1536]{3,2,1,0:T(8,128)(2,1)}, bf16[1,3,1,176,1536]{4,3,2,1,0:T(8,128)(2,1)}, f32[1536]{0:T(1024)}) custom-call(bf16[1,1,176,1536]{3,2,1,0:T(8,128)(2,1)S(1)} %get-tuple-element.6.refs_0_, bf16[1,3,1,176,1536]{4,3,2,1,0:T(8,128)(2,1)S(1)} %get-tuple-element.7.refs_1_, f32[1536]{0:T(1024)S(1)} %bitcast.2), custom_call_target="tpu_custom_call" | custom-call | tf_op jit(solution)/shard_map/pallas_call | solution.py:533

commit v5 on v3

--- a/solution.py
+++ b/solution.py
@@ -69,6 +69,8 @@
     round_recv,
     total_sems,
     small_sems,
+    entered,
+    known,
 ):
     z_size, dp_size, x_size, y_size = sizes
     core = lax.axis_index("grp")
@@ -263,9 +265,12 @@
             copy.start()
 
     barrier = pltpu.get_barrier_semaphore()
-    near = [{"seq": base + partners[k]} for k in (1, 2, 3)] + [other_core]
-    for peer in near:
-        pl.semaphore_signal(barrier, inc=1, device_id=peer, device_id_type=MESH)
+
+    def greet(peer, semaphore=barrier):
+        pl.semaphore_signal(semaphore, inc=1, device_id=peer, device_id_type=MESH)
+
+    def greet_partner(k, semaphore=barrier):
+        greet({"seq": base + partners[k]}, semaphore)
 
     @pl.when(core == 0)
     def _():
@@ -274,18 +279,58 @@
             far += [device(lax.rem(place + ahead, number)) for ahead in range(1, number)]
         if y_size == 2:
             far += [{"seq": ring_base + (1 - y_place) * GROUP + k} for k in range(GROUP)]
+        for k in (1, 2, 3):
+            greet_partner(k)
         for peer in far:
-            pl.semaphore_signal(barrier, inc=1, device_id=peer, device_id_type=MESH)
-        pl.semaphore_wait(barrier, len(near) + len(far))
+            greet(peer)
+        pl.semaphore_wait(barrier, GROUP + len(far))
+        greet(other_core, entered)
+        for head in range(heads - 1):
+            for k in (2, 3, 1):
+                for copy in in_pair(head, k):
+                    copy.start()
 
     @pl.when(core == 1)
     def _():
-        pl.semaphore_wait(barrier, len(near))
-
-    for head in range(heads - 1):
-        for k in (2, 3, 1):
-            for copy in in_pair(head, k):
+        greet_partner(2)
+        greet(other_core)
+
+        @pl.when(member == 0)
+        def _():
+            greet_partner(1)
+
+        @pl.when(member == 1)
+        def _():
+            pl.semaphore_wait(barrier, 2)
+
+        @pl.when(member != 1)
+        def _():
+            pl.semaphore_wait(barrier, 1)
+
+        for head in range(heads - 1):
+            for copy in in_pair(head, 2):
                 copy.start()
+
+        @pl.when(member == 1)
+        def _():
+            greet_partner(1, known)
+            pl.semaphore_wait(known, 1)
+            greet_partner(2, known)
+
+        @pl.when(member == 0)
+        def _():
+            pl.semaphore_wait(known, 1)
+            greet_partner(1, known)
+            greet_partner(2, known)
+
+        @pl.when(member >= 2)
+        def _():
+            pl.semaphore_wait(known, 1)
+
+        for head in range(heads - 1):
+            for k in (3, 1):
+                for copy in in_pair(head, k):
+                    copy.start()
 
     for copy in small:
         copy.wait()
@@ -337,6 +382,10 @@
 
         for k in (2, 3, 1, 0):
             out_pair(head, k, 0).start()
+
+    @pl.when(core == 1)
+    def _():
+        pl.semaphore_wait(entered, 1)
 
     for head in range(heads - 1):
         arrive(head)
@@ -521,6 +570,8 @@
             dma((3, places)),
             dma((2,)),
             dma((3,)),
+            pltpu.SemaphoreType.REGULAR,
+            pltpu.SemaphoreType.REGULAR,
         ],
         compiler_params=pltpu.CompilerParams(
             collective_id=0, has_side_effects=True, vmem_limit_bytes=44 * 1024 * 1024

time: 102 us -> 102 us (level)
  no operation moved by 1% of the time
where the time goes in v5:
time: 102 us
  Pallas kernels  101 us (99%)
    pallas_call x1, Pallas kernels, per_device(): pl.pallas_call(functools.partial(kernel, heads, (z_size, dp_size, x_size,...  99.8 us

profile of v5, /device:TPU:1, one launch (start us, length us, event | category | flops | bytes accessed | tf_op | source)
XLA Modules:
  0.0 101.8 jit_solution(9606968337354163578)
XLA Ops:
  0.6 99.8 %shard_map.76 = (bf16[1,1,176,1536]{3,2,1,0:T(8,128)(2,1)S(1)}, bf16[1,3,1,176,1536]{4,3,2,1,0:T(8,128)(2,1)S(1)}, f32[12,128]{1,0:T(8,128)S(1)}) custom-call(bf16[1,3,1,176,1536]{4,3,2,1,0:T(8,128)(2,1)} %qkv.1, bf16[1,1,176,1536]{3,2,1,0:T(8,128)(2,1)} %cot.1, f32[12,128]{1,0:T(8,128)} %bitcast.3, s32[1,32,704]{2,1,0:T(8,128)} %tile_map.1, s32[1,32]{1,0:T(1,128)} %text_count.1), custom_call_target="tpu_custom_call" | custom-call | tf_op jit(solution)/shard_map/pallas_call | solution.py:535
  100.4 1.4 %shard_map.77 = (bf16[1,1,176,1536]{3,2,1,0:T(8,128)(2,1)}, bf16[1,3,1,176,1536]{4,3,2,1,0:T(8,128)(2,1)}, f32[1536]{0:T(1024)}) custom-call(bf16[1,1,176,1536]{3,2,1,0:T(8,128)(2,1)S(1)} %get-tuple-element.6.refs_0_, bf16[1,3,1,176,1536]{4,3,2,1,0:T(8,128)(2,1)S(1)} %get-tuple-element.7.refs_1_, f32[1536]{0:T(1024)S(1)} %bitcast.2), custom_call_target="tpu_custom_call" | custom-call | tf_op jit(solution)/shard_map/pallas_call | solution.py:586
